TPU v7x, 512 devices: a whole 4x8x8 slice. The times are simulated.
512 devices in a mesh: tok: 16 (over z_hi, y), row: 4 (over x), col: 8 (over z_lo, core).
Axes of the slice: x: 4, y: 8, z: 8 (z_hi: 2, z_lo: 4; z = z_hi * 4 + z_lo), core: 2. Of those that a mesh axis runs over, the one named last changes fastest.
Arguments:
- inputs: bfloat16 [640, 6144], P('tok', 'row'), may hold values from -6 to 6
- pre_act: bfloat16 [640, 49152], P('row', ('tok', 'col')), may hold values from -9 to 9
- w_in: bfloat16 [6144, 49152], P('row', ('tok', 'col')), may hold values from -0.078125 to 0.078125
- w_out: bfloat16 [49152, 6144], P(('tok', 'col'), 'row'), may hold values from -0.02734375 to 0.02734375
- out_grad: bfloat16 [640, 6144], P(('tok', 'col'), 'row'), may hold values from -1.1953125 to 1.1953125
Outputs:
- input_grad: bfloat16 [640, 6144], P(('tok', 'col'), 'row')
- w_in_grad: bfloat16 [6144, 49152], P('row', ('tok', 'col'))
- bias_in_grad: float32 [49152], P(('tok', 'col'))
- w_out_grad: bfloat16 [49152, 6144], P(('tok', 'col'), 'row')
- bias_out_grad: float32 [6144], P('row')
All inputs are finite; a program needn't handle non-finite values.
Results may differ from a plain program's by a relative error of at most 0.018.
Values may be sent and summed in bfloat16 or wider, within the bound.
A program may use at most 64 MiB of HBM per device.

v0:
```python
import math

import jax
import jax.numpy as jnp
from jax import lax
from jax.sharding import PartitionSpec as P

root_two_pi = math.sqrt(2.0 / math.pi)


def gelu_parts(values):
    cubic = values * values * values
    inner = root_two_pi * (values + 0.044715 * cubic)
    tangent = jnp.tanh(inner)
    result = 0.5 * values * (1.0 + tangent)
    slope = 0.5 * (1.0 + tangent) + 0.5 * values * (1.0 - tangent * tangent) * root_two_pi * (
        1.0 + 3.0 * 0.044715 * values * values
    )
    return (result, slope)


def body(inputs, pre_act, w_in, w_out, out_grad):
    grad_all = lax.all_gather(out_grad, ("tok", "col"), axis=0, tiled=True)
    pre_all = lax.all_gather(pre_act, "row", axis=0, tiled=True)
    result, slope_all = gelu_parts(pre_all.astype(jnp.float32))
    hidden = result.astype(jnp.bfloat16)
    w_out_grad = lax.dot_general(
        hidden, grad_all, (((0,), (0,)), ((), ())), preferred_element_type=jnp.float32
    ).astype(jnp.bfloat16)
    bias_out_grad = jnp.sum(grad_all, axis=0, dtype=jnp.float32)
    partial_grad = lax.dot_general(
        grad_all, w_out, (((1,), (1,)), ((), ())), preferred_element_type=jnp.float32
    )
    summed = lax.psum(partial_grad.astype(jnp.bfloat16), "row").astype(jnp.float32)
    act_grad = (summed * slope_all).astype(jnp.bfloat16)
    bias_in_grad = jnp.sum(act_grad, axis=0, dtype=jnp.float32)
    rows_grad = act_grad
    w_in_grad = lax.dot_general(
        lax.all_gather(inputs, "tok", axis=0, tiled=True),
        rows_grad,
        (((0,), (0,)), ((), ())),
        preferred_element_type=jnp.float32,
    ).astype(jnp.bfloat16)
    rows_grad = act_grad
    summed_input = lax.psum_scatter(
        lax.dot_general(
            rows_grad, w_in, (((1,), (1,)), ((), ())), preferred_element_type=jnp.float32
        ),
        ("tok", "col"),
        scatter_dimension=0,
        tiled=True,
    )
    input_grad = summed_input.astype(jnp.bfloat16)
    return (input_grad, w_in_grad, bias_in_grad, w_out_grad, bias_out_grad)


def solution(mesh):
    placed = (
        P("tok", "row"),
        P("row", ("tok", "col")),
        P("row", ("tok", "col")),
        P(("tok", "col"), "row"),
        P(("tok", "col"), "row"),
    )
    return jax.shard_map(
        body,
        mesh=mesh,
        in_specs=placed,
        out_specs=(
            P(("tok", "col"), "row"),
            P("row", ("tok", "col")),
            P(("tok", "col")),
            P(("tok", "col"), "row"),
            P("row"),
        ),
        check_vma=False,
    )
```

profile of v0, /device:TPU:36, one launch (start us, length us, event | category | flops | bytes accessed | tf_op | source)
XLA Modules:
  0.0 932.0 jit_solution(7753179458772569972)
XLA Ops:
  8.0 0.0 copy-start
  8.0 0.0 all-gather.6.cloned.1.call-start
  8.1 0.7 all-gather.6.cloned.1.call-update
  8.7 0.0 all-reduce.4.cloned.1.call-start
  8.8 222.6 %all-gather.6.cloned.1.call-done = bf16[128,5,1536]{2,1,0:T(8,128)(2,1)} async-done(((bf16[1,5,1536]{2,1,0:T(8,128)(2,1)}), bf16[128,5,1536]{2,1,0:T(8,128)(2,1)}) %all-gather.6.cloned.1.call-update) | async-done | bytes 1966096 | tf_op jit(solution)/shard_map/all_gather | solution.py:23
  231.4 3.0 reshape.11
  234.4 0.0 copy-start.2
  234.4 3.3 convolution_convert_fusion.2
  237.7 0.0 all-reduce.4.cloned.1.call-update
  237.7 0.0 all-gather.4.cloned.1.call-start
  237.8 0.5 all-gather.4.cloned.1.call-update
  238.3 1.3 dynamic-slice
  240.2 0.0 copy-done.2
  240.2 11.5 %all_gather.10 = bf16[640,384]{1,0:T(8,128)(2,1)S(1)} all-gather(bf16[160,384]{1,0:T(8,128)(2,1)S(1)} %copy-done.2), channel_id=1, replica_groups=mesh['tok'=16,'row'=4,'col'=8] {'row'}, dimensions={0}, use_global_device_ids=true | all-gather | bytes 614400 | tf_op jit(solution)/shard_map/all_gather | solution.py:24
  251.7 0.0 copy-start.1
  251.7 0.9 convert_reduce_fusion
  252.7 0.0 copy-done.1
  252.7 2.2 convolution_convert_fusion
  254.8 37.7 %all-reduce.4.cloned.1.call-done = bf16[640,384]{1,0:T(8,128)(2,1)} async-done(((bf16[640,384]{1,0:T(8,128)(2,1)}), bf16[640,384]{1,0:T(8,128)(2,1)}) %all-reduce.4.cloned.1.call-update) | async-done | bytes 491536 | tf_op jit(solution)/shard_map/psum | solution.py:34
  292.5 2.5 convert_reduce_fusion.1
  295.0 50.9 %all-gather.4.cloned.1.call-done = bf16[640,1536]{1,0:T(8,128)(2,1)} async-done(((bf16[40,1536]{1,0:T(8,128)(2,1)}), bf16[640,1536]{1,0:T(8,128)(2,1)}) %all-gather.4.cloned.1.call-update) | async-done | bytes 1966096 | tf_op jit(solution)/shard_map/all_gather | solution.py:39
  345.9 2.6 fusion
  348.6 1.4 copy.12
  350.0 0.0 copy-done
  350.0 3.1 fusion.23
  353.1 570.9 %all-reduce.5 = bf16[640,1536]{1,0:T(8,128)(2,1)S(1)} all-reduce(f32[640,1536]{1,0:T(8,128)} %fusion.23), channel_id=2, replica_groups=mesh['tok'=16,'row'=4,'col'=8] {'tok','col'}, use_global_device_ids=true, to_apply=%region_1.0.clone | all-reduce | flops 983040 | bytes 5898240
  924.0 0.6 dynamic-slice_convert_fusion
Async XLA Ops:
  8.0 342.0 %copy-start = (bf16[1536,384]{1,0:T(8,128)(2,1)S(1)}, bf16[1536,384]{1,0:T(8,128)(2,1)}, u32[]{:S(2)}) copy-start(bf16[1536,384]{1,0:T(8,128)(2,1)} %param.7) | copy-start | bytes 3538948
  8.0 223.4 %all-gather.6.cloned.1.call-start = ((), (), s32[]{:S(2)}) async-start(), calls=%async_computation.2 | async-start | bytes 3170304 | tf_op jit(solution)/shard_map/all_gather | solution.py:23
  8.7 283.8 %all-reduce.4.cloned.1.call-start = ((), (), s32[]{:S(2)}) async-start(), calls=%async_computation | async-start | bytes 983040 | tf_op jit(solution)/shard_map/psum | solution.py:34
  234.4 5.8 copy-start.2
  237.7 108.2 %all-gather.4.cloned.1.call-start = ((), (), s32[]{:S(2)}) async-start(), calls=%async_computation.1 | async-start | bytes 2088960 | tf_op jit(solution)/shard_map/all_gather | solution.py:39
  251.7 0.9 copy-start.1
Sparse Core Ops, SparseCore 0:
  11.0 220.3 all-gather.5
  237.8 54.6 all-reduce.3
Sparse Core Ops, SparseCore 1:
  241.8 104.0 all-gather.3
where the time goes:
time: 932 us
  blocking collectives  582 us (62%)
  waiting for transfers between devices  312 us (33%)
  between operations  16.2 us (2%)
  matrix products  11.2 us (1%)
    unnamed x1, blocking collectives  571 us
    all_gather x1, waiting for transfers between devices, body(): grad_all = lax.all_gather(out_grad, ('tok', 'col'), axis=0, tiled=True)  223 us
    all_gather x1, waiting for transfers between devices, body(): lax.all_gather(inputs, 'tok', axis=0, tiled=True)  50.9 us
    psum x1, waiting for transfers between devices, body(): lax.psum(partial_grad.astype(jnp.bfloat16), 'row').astype(jnp.float32)  37.7 us
  transfers between devices with their start and end apart: 3, of which 3 were waited for; matrix products, arithmetic and copies ran while one was open for 1% of the time, Pallas kernels for 0%

commit v1 on v0

v1 whole, which is shorter than its diff:
```python
import functools
import math

import jax
import jax.numpy as jnp
import numpy as np
from jax import lax
from jax.experimental import pallas as pl
from jax.experimental.pallas import tpu as pltpu
from jax.sharding import PartitionSpec as P

MESH = pl.DeviceIdType.MESH
F32 = jnp.float32
BF16 = jnp.bfloat16
root_two_pi = math.sqrt(2.0 / math.pi)
T = 5
ZL = 4
STEPS = 3


def gelu_parts(values):
    cubic = values * values * values
    inner = root_two_pi * (values + 0.044715 * cubic)
    tangent = jnp.tanh(inner)
    result = 0.5 * values * (1.0 + tangent)
    slope = 0.5 * (1.0 + tangent) + 0.5 * values * (1.0 - tangent * tangent) * root_two_pi * (
        1.0 + 3.0 * 0.044715 * values * values
    )
    return (result, slope)


def nt(a, b):
    return lax.dot_general(a, b, (((1,), (1,)), ((), ())), preferred_element_type=F32)


def tn(a, b):
    return lax.dot_general(a, b, (((0,), (0,)), ((), ())), preferred_element_type=F32)


def nn(a, b):
    return lax.dot_general(a, b, (((1,), (0,)), ((), ())), preferred_element_type=F32)


def kernel(
    cfg,
    x_ref, pre_hbm, w_in_hbm, w_out_hbm, og_ref, swap_hbm, unfold_hbm, fold_hbm,
    ig_ref, wi_hbm, bi_ref, wo_hbm, bo_ref,
    w_in, w_out, swap, unfold, fold, sb, rb, gg, ii, gy, pre, hid, slope, pb, pr, act, actz, sx, sr, sc, tb, tr,
    fb, qq, wi, wo,
    loc, outs, s_pre, r_pre, s1, r1, sg, rg, si, ri, sp, rp, sa, ra, ss, rs, st, rt, sq, rq,
):
    N, X, zl_n = cfg["N"], cfg["X"], cfg["ZL"]
    U = 2 * N * T
    H = cfg["H"]
    W = cfg["W"]
    HF = STEPS * W
    M = N * U
    RB = M // X
    UR = RB // U
    TK = 2 * zl_n * T

    tok, x, col = lax.axis_index("tok"), lax.axis_index("row"), lax.axis_index("col")
    y, c = lax.rem(tok, N), lax.rem(col, 2)
    z = (tok // N) * zl_n + col // 2
    b = y + c * (z - y)
    a = z + c * (y - z)

    def dev(yy, zz, cc, xx=x):
        return ((zz // zl_n) * N + yy, xx, lax.rem(zz, zl_n) * 2 + cc)

    def bdev(bb):
        return dev(y + (1 - c) * (bb - y), z + c * (bb - z), c)

    def adev(aa, cc):
        return dev(y + c * (aa - y), z + (1 - c) * (aa - z), cc)

    mate = dev(y, z, 1 - c)

    def rcopy(src, dst, ssem, rsem, to):
        return pltpu.make_async_remote_copy(
            src_ref=src, dst_ref=dst, send_sem=ssem, recv_sem=rsem, device_id=to, device_id_type=MESH
        )

    def got(dst, rsem):
        rcopy(dst, dst, rsem, rsem, mate).wait_recv()

    def sent(src, ssem):
        rcopy(src, src, ssem, ssem, mate).wait_send()

    loads = [
        pltpu.make_async_copy(unfold_hbm, unfold, loc.at[0]),
        pltpu.make_async_copy(pre_hbm, pre.at[x], loc.at[1]),
        pltpu.make_async_copy(swap_hbm, swap, loc.at[2]),
        pltpu.make_async_copy(w_out_hbm, w_out, loc.at[3]),
        pltpu.make_async_copy(w_in_hbm, w_in, loc.at[4]),
        pltpu.make_async_copy(fold_hbm, fold, loc.at[5]),
    ]
    for load in loads:
        load.start()

    bar = pltpu.get_barrier_semaphore()

    def greet(yy, zz, cc, xx=x):
        pl.semaphore_signal(bar, inc=1, device_id=dev(yy, zz, cc, xx), device_id_type=MESH)

    greet(y, z, 1 - c)
    for d in range(1, X):
        greet(y, z, c, lax.rem(x + d, X))

    def greet_step(d, _):
        yy, zz = lax.rem(y + d, N), lax.rem(z + d, N)
        for cc in range(2):
            greet(yy, z, cc)
            greet(y, zz, cc)
        return 0

    lax.fori_loop(1, N, greet_step, 0)

    og = og_ref[...].astype(F32)
    xall = x_ref[...].astype(F32)
    xs = xall[0:T]
    for k in range(1, 2 * zl_n):
        xs = jnp.where(col == k, xall[T * k : T * k + T], xs)
    pad = jnp.zeros((1, W), F32)
    for h in range(2):
        rows = []
        for v in (og, xs):
            rows += [v[:, h * HF + j * W : h * HF + (j + 1) * W] for j in range(STEPS)] + [pad]
        sb[h] = jnp.concatenate(rows, axis=0).astype(BF16)

    pl.semaphore_wait(bar, 1 + (X - 1) + 4 * (N - 1))

    @pl.when(c == 0)
    def _():
        rb[2 * z] = sb[0]
        rcopy(sb.at[1], rb.at[2 * y], s1.at[0], r1.at[0], mate).start()

    @pl.when(c == 1)
    def _():
        rb[2 * y + 1] = sb[1]
        rcopy(sb.at[0], rb.at[2 * z + 1], s1.at[0], r1.at[0], mate).start()

    def small(d, _):
        yy, zz = lax.rem(y + d, N), lax.rem(z + d, N)
        rcopy(sb.at[0], rb.at[2 * z + c], s1.at[0], r1.at[0], dev(y, zz, 0)).start()
        rcopy(sb.at[1], rb.at[2 * y + c], s1.at[0], r1.at[0], dev(yy, z, 1)).start()
        return 0

    lax.fori_loop(1, N, small, 0)

    for d in range(1, X):
        rcopy(pre_hbm, pre.at[x], s_pre.at[0], r_pre.at[0], dev(y, z, c, lax.rem(x + d, X))).start()

    loads[0].wait()
    got(rb.at[pl.ds(0, 2 * N - 1)], r1.at[0])
    unit = nn(unfold[...], rb[...].reshape(2 * N * 32, W))
    own = c * N + b
    for k, buf in enumerate((gg, ii)):
        for j in range(STEPS):
            at = (k * STEPS + j) * U
            buf[own, :, j * W : (j + 1) * W] = unit[at : at + U].astype(BF16)

    for buf, ssem, rsem in ((gg, sg, rg), (ii, si, ri)):

        def large(d, _, buf=buf, ssem=ssem, rsem=rsem):
            bb = lax.rem(b + d, N)
            rcopy(buf.at[own], buf.at[own], ssem.at[0], rsem.at[own], bdev(bb)).start()
            return 0

        lax.fori_loop(1, N, large, 0)
        rcopy(buf.at[own], buf.at[own], ssem.at[0], rsem.at[own], mate).start()

    loads[1].wait()
    got(pre.at[pl.ds(0, X - 1)], r_pre.at[0])
    for r in range(X):
        for q in range(RB // TK):
            g = r * (RB // TK) + q
            zh, yy = g // N, g % N
            at = yy * U + zh * TK
            result, grade = gelu_parts(pre[r].astype(F32)[q * TK : q * TK + TK])
            hid[at : at + TK] = result
            slope[at : at + TK] = grade

    def forward(buf, ssem, rsem):
        def step(d, _):
            at = c * N + lax.rem(b + d, N)
            got(buf.at[at], rsem.at[at])
            rcopy(buf.at[at], buf.at[at], ssem.at[0], rsem.at[at], mate).start()
            return 0

        lax.fori_loop(1, N, step, 0)

    def from_mate(buf, rsem):
        def step(k, _):
            at = (1 - c) * N + k
            got(buf.at[at], rsem.at[at])
            return 0

        lax.fori_loop(0, N, step, 0)

    forward(gg, sg, rg)
    loads[2].wait()
    loads[3].wait()
    from_mate(gg, rg)

    for d in range(1, X + 1):
        r = lax.rem(x + d, X)
        g1 = gg[pl.ds(N, N)].reshape(M, HF)
        mine = pl.ds(pl.multiple_of(r * RB, 16), RB)
        g1y = nn(swap[mine], g1).astype(BF16)
        gy[mine] = g1y
        g0 = gg[pl.ds(r * UR, UR)].reshape(RB, HF)
        part = nt(g0, w_out[:, :HF]) + nt(g1y, w_out[:, HF:])
        if d < X:
            pb[r] = part.astype(BF16)
            rcopy(pb.at[r], pr.at[x], sp.at[0], rp.at[0], dev(y, z, c, r)).start()
        else:
            pr[x] = part.astype(BF16)

    forward(ii, si, ri)

    hidden = hid[...].astype(BF16)
    wo[:, :HF] = tn(hidden, gg[pl.ds(0, N)].reshape(M, HF)).astype(BF16)
    bo = [jnp.sum(gg[pl.ds(0, N)].reshape(M, HF).astype(F32), axis=0, keepdims=True)]
    wo[:, HF:] = tn(hidden, gy[...]).astype(BF16)
    bo += [jnp.sum(gy[...].astype(F32), axis=0, keepdims=True)]
    bo_ref[...] = jnp.concatenate(bo, axis=1)
    put_wo = pltpu.make_async_copy(wo, wo_hbm, outs.at[0])
    put_wo.start()

    got(pr.at[pl.ds(0, X - 1)], rp.at[0])
    total = pr[0].astype(F32)
    for r in range(1, X):
        total = total + pr[r].astype(F32)
    mine = pl.ds(pl.multiple_of(x * RB, 16), RB)
    act[x] = (total * slope[mine]).astype(BF16)
    for d in range(1, X):
        rcopy(act.at[x], act.at[x], sa.at[0], ra.at[0], dev(y, z, c, lax.rem(x + d, X))).start()

    loads[4].wait()
    loads[5].wait()
    got(act.at[pl.ds(0, X - 1)], ra.at[0])
    acty = act[...].reshape(M, H)
    actz[0] = acty
    actz[1] = nn(swap[...], acty).astype(BF16)

    mate_b = z + c * (y - z)
    for i in range(X):
        k = lax.rem(mate_b // UR + i, X)
        rows = pl.ds(pl.multiple_of(k * RB, 16), RB)
        part = nt(actz[1 - c, rows], w_in[1 - c]).astype(BF16)
        sx[pl.ds(k * UR, UR)] = part.reshape(UR, U, HF)
        rcopy(sx.at[pl.ds(k * UR, UR)], sr.at[pl.ds(k * UR, UR)], ss.at[0], rs.at[k], mate).start()

    bi_ref[...] = jnp.sum(acty.astype(F32), axis=0, keepdims=True)

    for i in range(X):
        k = lax.rem(b // UR + i, X)
        rows = pl.ds(pl.multiple_of(k * RB, 16), RB)
        part = nt(actz[c, rows], w_in[c])
        got(sr.at[pl.ds(k * UR, UR)], rs.at[k])
        part = part.reshape(UR, U, HF) + sr[pl.ds(k * UR, UR)].astype(F32)
        sc[pl.ds(k * UR, UR)] = part
        tb[pl.ds(k * UR, UR)] = part.astype(BF16)
        for u in range(UR):
            bb = k * UR + u

            @pl.when(bb != b)
            def _(bb=bb):
                rcopy(tb.at[bb], tr.at[b], st.at[0], rt.at[0], bdev(bb)).start()

    from_mate(ii, ri)
    for h in range(2):
        wi[h] = tn(ii[pl.ds(h * N, N)].reshape(M, HF), actz[h]).astype(BF16)
    put_wi = pltpu.make_async_copy(wi, wi_hbm, outs.at[1])
    put_wi.start()

    got(tr.at[pl.ds(0, N - 1)], rt.at[0])
    total = sc[b]
    for d in range(1, N):
        total = total + tr[lax.rem(b + d, N)].astype(F32)
    total = total.astype(BF16)
    stack = jnp.concatenate([total[:, j * W : (j + 1) * W] for j in range(STEPS)], axis=0)
    fb[...] = nn(fold[...], stack).astype(BF16).reshape(2 * N, 16, W)
    qq[own_slot(c, a, N)] = fb[2 * a + c]
    rcopy(fb.at[2 * a + 1 - c], qq.at[own_slot(c, a, N)], sq.at[0], rq.at[0], mate).start()

    def last(d, _):
        aa = lax.rem(a + d, N)
        for k in range(2):
            cc = lax.rem(c + k, 2)
            rcopy(fb.at[2 * aa + cc], qq.at[own_slot(c, a, N)], sq.at[0], rq.at[0], adev(aa, cc)).start()
        return 0

    lax.fori_loop(1, N, last, 0)
    got(qq.at[pl.ds(0, 2 * N - 1)], rq.at[0])
    for h in range(2):
        rows = jnp.sum(qq[pl.ds(h * N, N)].astype(F32), axis=0)
        for j in range(STEPS):
            at = h * HF + j * W
            ig_ref[:, at : at + W] = rows[T * j : T * j + T].astype(BF16)

    sent(rb.at[pl.ds(0, 2 * N - 1)], s1.at[0])
    sent(pre.at[pl.ds(0, X - 1)], s_pre.at[0])
    sent(gg.at[pl.ds(0, 2 * N - 1)], sg.at[0])
    sent(ii.at[pl.ds(0, 2 * N - 1)], si.at[0])
    sent(pb.at[pl.ds(0, X - 1)], sp.at[0])
    sent(act.at[pl.ds(0, X - 1)], sa.at[0])
    sent(sx, ss.at[0])
    sent(tb.at[pl.ds(0, N - 1)], st.at[0])
    sent(qq.at[pl.ds(0, 2 * N - 1)], sq.at[0])
    put_wo.wait()
    put_wi.wait()


def own_slot(c, a, n):
    return c * n + a


def tables(n, u):
    m = n * u
    q = 2 * T
    r = np.arange(m)
    swap = np.zeros((m, m), np.float32)
    swap[r, ((r % u) // q) * u + (r // u) * q + r % q] = 1
    unfold = np.zeros((2 * STEPS * u, 2 * n * 32), np.float32)
    fold = np.zeros((2 * n * 16, STEPS * u), np.float32)
    for j in range(STEPS):
        for t in range(u):
            for k in range(2):
                unfold[(k * STEPS + j) * u + t, (t // T) * 32 + k * 16 + T * j + t % T] = 1
            fold[(t // T) * 16 + T * j + t % T, j * u + t] = 1
    return swap, unfold, fold


def solution(mesh):
    X = mesh.shape["row"]
    zl_n = mesh.shape["col"] // 2
    N = math.isqrt(mesh.shape["tok"] * zl_n)
    U = 2 * N * T
    M = N * U

    def body(inputs, pre_act, w_in, w_out, out_grad):
        F, H = w_in.shape
        W = F // (2 * STEPS)
        HF = F // 2
        RB = M // X
        cfg = {"N": N, "X": X, "ZL": zl_n, "H": H, "W": W}
        consts = [jnp.asarray(t, BF16) for t in tables(N, U)]
        vm = pl.BlockSpec(memory_space=pltpu.VMEM)
        hbm = pl.BlockSpec(memory_space=pl.ANY)
        dma = pltpu.SemaphoreType.DMA
        outs = pl.pallas_call(
            functools.partial(kernel, cfg),
            out_shape=(
                jax.ShapeDtypeStruct((T, F), BF16),
                jax.ShapeDtypeStruct((2, HF, H), BF16),
                jax.ShapeDtypeStruct((1, H), F32),
                jax.ShapeDtypeStruct((H, F), BF16),
                jax.ShapeDtypeStruct((1, F), F32),
            ),
            in_specs=[vm, hbm, hbm, hbm, vm, hbm, hbm, hbm],
            out_specs=(vm, hbm, vm, hbm, vm),
            scratch_shapes=[
                pltpu.VMEM((2, HF, H), BF16),
                pltpu.VMEM((H, F), BF16),
                pltpu.VMEM(consts[0].shape, BF16),
                pltpu.VMEM(consts[1].shape, BF16),
                pltpu.VMEM(consts[2].shape, BF16),
                pltpu.VMEM((2, 32, W), BF16),
                pltpu.VMEM((2 * N, 32, W), BF16),
                pltpu.VMEM((2 * N, U, HF), BF16),
                pltpu.VMEM((2 * N, U, HF), BF16),
                pltpu.VMEM((M, HF), BF16),
                pltpu.VMEM((X, RB, H), BF16),
                pltpu.VMEM((M, H), F32),
                pltpu.VMEM((M, H), F32),
                pltpu.VMEM((X, RB, H), BF16),
                pltpu.VMEM((X, RB, H), BF16),
                pltpu.VMEM((X, RB, H), BF16),
                pltpu.VMEM((2, M, H), BF16),
                pltpu.VMEM((N, U, HF), BF16),
                pltpu.VMEM((N, U, HF), BF16),
                pltpu.VMEM((N, U, HF), F32),
                pltpu.VMEM((N, U, HF), BF16),
                pltpu.VMEM((N, U, HF), BF16),
                pltpu.VMEM((2 * N, 16, W), BF16),
                pltpu.VMEM((2 * N, 16, W), BF16),
                pltpu.VMEM((2, HF, H), BF16),
                pltpu.VMEM((H, F), BF16),
                dma((6,)), dma((2,)),
                dma((1,)), dma((1,)),
                dma((1,)), dma((1,)),
                dma((1,)), dma((2 * N,)),
                dma((1,)), dma((2 * N,)),
                dma((1,)), dma((1,)),
                dma((1,)), dma((1,)),
                dma((1,)), dma((X,)),
                dma((1,)), dma((1,)),
                dma((1,)), dma((1,)),
            ],
            compiler_params=pltpu.CompilerParams(
                collective_id=0, has_side_effects=True, vmem_limit_bytes=60 * 1024 * 1024
            ),
        )(inputs, pre_act, w_in.reshape(2, HF, H), w_out, out_grad, *consts)
        ig, wi, bi, wo, bo = outs
        return (ig, wi.reshape(F, H), bi.reshape(H), wo, bo.reshape(F))

    return jax.shard_map(
        body,
        mesh=mesh,
        in_specs=(
            P("tok", "row"),
            P("row", ("tok", "col")),
            P("row", ("tok", "col")),
            P(("tok", "col"), "row"),
            P(("tok", "col"), "row"),
        ),
        out_specs=(
            P(("tok", "col"), "row"),
            P("row", ("tok", "col")),
            P(("tok", "col")),
            P(("tok", "col"), "row"),
            P("row"),
        ),
        check_vma=False,
    )
```

time: 932 us -> 89.2 us (0.10)
  the two profiles are of different devices: /device:TPU:36 before, /device:TPU:1 now
where the time goes in v1:
time: 89.2 us; the launch traced here: 89 us
  Pallas kernels  80.9 us (91%)
  local copies, waits for them, and re-layouts  4.86 us (5%)
  other arithmetic  2.57 us (3%)
    pallas_call x1, Pallas kernels, body(): pl.pallas_call(functools.partial(kernel, cfg), out_shape=(jax.ShapeDtypeS...  80.9 us
    unnamed x5, local copies, waits for them, and re-layouts  4.86 us
    pallas_call x2, other arithmetic, body(): pl.pallas_call(functools.partial(kernel, cfg), out_shape=(jax.ShapeDtypeS...  2.57 us

profile of v1, /device:TPU:1, one launch (start us, length us, event | category | flops | bytes accessed | tf_op | source)
XLA Modules:
  0.0 89.0 jit_solution(12973767626941587703)
XLA Ops:
  0.6 80.9 %shard_map.119 = (bf16[5,1536]{1,0:T(8,128)(2,1)}, bf16[2,768,384]{2,1,0:T(8,128)(2,1)}, f32[1,384]{1,0:T(1,128)}, bf16[384,1536]{1,0:T(8,128)(2,1)}, f32[1,1536]{1,0:T(1,128)}) custom-call(bf16[40,1536]{1,0:T(8,128)(2,1)} %x_ref.1, bf16[160,384]{1,0:T(8,128)(2,1)} %pre_hbm.1, bf16[2,768,384]{2,1,0:T(8,128)(2,1)} %bitcast.3, bf16[384,1536]{1,0:T(8,128)(2,1)} %w_out_hbm.1, ...), custom_call_target="tpu_custom_call" | custom-call | tf_op jit(solution)/shard_map/pallas_call | solution.py:353
  81.5 1.3 %reduce.1 = f32[1536]{0:T(1024)} reduce(f32[1,1536]{1,0:T(1,128)} %get-tuple-element.14, f32[]{:T(128)} %constant.11), dimensions={0}, to_apply=%get-tuple-element.14.reduce_sub_computation | reduce | bytes 12292 | tf_op jit(solution)/shard_map/pallas_call | solution.py:353
  82.8 1.3 %reduce = f32[384]{0:T(512)} reduce(f32[1,384]{1,0:T(1,128)} %get-tuple-element.12, f32[]{:T(128)} %constant.11), dimensions={0}, to_apply=%get-tuple-element.12.reduce_sub_computation | reduce | bytes 3076 | tf_op jit(solution)/shard_map/pallas_call | solution.py:353
  84.1 1.3 %copy.16 = bf16[5,1536]{1,0:T(8,128)(2,1)} copy(bf16[5,1536]{1,0:T(8,128)(2,1)} %get-tuple-element.20) | data formatting | bytes 30720
  85.4 0.0 copy-start
  85.5 2.5 %copy.17 = bf16[1536,384]{1,0:T(8,128)(2,1)} copy(bf16[1536,384]{1,0:T(8,128)(2,1)} %bitcast.2) | data formatting | bytes 2359296
  87.9 0.0 copy-done
  88.0 1.0 %copy.18 = bf16[384,1536]{1,0:T(8,128)(2,1)} copy(bf16[384,1536]{1,0:T(8,128)(2,1)S(1)} %copy-done) | data formatting | bytes 2359296
Async XLA Ops:
  85.4 2.5 %copy-start = (bf16[384,1536]{1,0:T(8,128)(2,1)S(1)}, bf16[384,1536]{1,0:T(8,128)(2,1)}, u32[]{:S(2)}) copy-start(bf16[384,1536]{1,0:T(8,128)(2,1)} %get-tuple-element.23) | copy-start | bytes 3538948

commit v2 on v1

v2 whole, which is shorter than its diff:
```python
import functools
import math

import jax
import jax.numpy as jnp
import numpy as np
from jax import lax
from jax.experimental import pallas as pl
from jax.experimental.pallas import tpu as pltpu
from jax.sharding import PartitionSpec as P

MESH = pl.DeviceIdType.MESH
F32 = jnp.float32
BF16 = jnp.bfloat16
root_two_pi = math.sqrt(2.0 / math.pi)
T = 5
ZL = 4
CHUNKS = 2
VM = 60 * 2**20
STEPS = 3


def gelu_parts(values):
    cubic = values * values * values
    inner = root_two_pi * (values + 0.044715 * cubic)
    tangent = jnp.tanh(inner)
    result = 0.5 * values * (1.0 + tangent)
    slope = 0.5 * (1.0 + tangent) + 0.5 * values * (1.0 - tangent * tangent) * root_two_pi * (
        1.0 + 3.0 * 0.044715 * values * values
    )
    return (result, slope)


def nt(a, b):
    return lax.dot_general(a, b, (((1,), (1,)), ((), ())), preferred_element_type=F32)


def tn(a, b):
    return lax.dot_general(a, b, (((0,), (0,)), ((), ())), preferred_element_type=F32)


def nn(a, b):
    return lax.dot_general(a, b, (((1,), (0,)), ((), ())), preferred_element_type=F32)


class Gather:
    def __init__(self, n, me, buf, slot, pieces, ssem, rsem, send, mate):
        self.n, self.me, self.buf, self.slot, self.pieces = n, me, buf, slot, pieces
        self.ssem, self.rsem, self.send, self.mate = ssem, rsem, send, mate

    def piece(self, unit, p):
        at, size = self.pieces[p]
        return self.buf.at[self.slot(unit), pl.ds(at, size)], self.rsem.at[self.slot(unit) * len(self.pieces) + p]

    def push(self, unit, p, to):
        ref, sem = self.piece(unit, p)
        self.send(ref, ref, self.ssem.at[0], sem, to).start()

    def of(self, way, far):
        half = (len(self.pieces) + 1) // 2
        every = range(len(self.pieces))
        return every if not far else (every[:half] if way > 0 else every[half:])

    def start(self):
        for p in range(len(self.pieces)):
            for way in (1, -1):
                if p in self.of(way, self.n == 2):
                    self.push(self.me, p, way)
        if self.mate:
            for p in range(len(self.pieces)):
                self.push(self.me, p, 0)

    def step(self, k):
        for p in range(len(self.pieces)):
            for way in (1, -1):
                if p in self.of(way, 2 * k == self.n):
                    unit = lax.rem(self.me - way * k + self.n, self.n)
                    ref, sem = self.piece(unit, p)
                    self.send(ref, ref, sem, sem, 0).wait_recv()
                    if 2 * k < self.n and p in self.of(way, 2 * k + 2 == self.n):
                        self.push(unit, p, way)
                    if self.mate:
                        self.push(unit, p, 0)


class Scatter:
    def __init__(self, n, me, own, out, land, pieces, ssem, rsem, send):
        self.n, self.me, self.own, self.out, self.land, self.pieces = n, me, own, out, land, pieces
        self.ssem, self.rsem, self.send = ssem, rsem, send

    def of(self, way, first):
        half = (len(self.pieces) + 1) // 2
        every = range(len(self.pieces))
        return every if not first else (every[:half] if way > 0 else every[half:])

    def place(self, way, s, p):
        at = (0 if way > 0 else self.n // 2) + s
        rows = pl.ds(*self.pieces[p])
        return self.out.at[at, rows], self.land.at[at, rows], self.rsem.at[at * len(self.pieces) + p]

    def arrived(self, way, s, p):
        _, land, sem = self.place(way, s, p)
        self.send(land, land, sem, sem, 0).wait_recv()
        return land[...].astype(F32)

    def step(self, s):
        for p in range(len(self.pieces)):
            for way in (1, -1):
                if p in self.of(way, s == 0):
                    unit = lax.rem(self.me + way * (self.n // 2 - s) + self.n, self.n)
                    value = self.own[unit, pl.ds(*self.pieces[p])]
                    if s and p in self.of(way, s == 1):
                        value = value + self.arrived(way, s - 1, p)
                    out, land, sem = self.place(way, s, p)
                    out[...] = value.astype(BF16)
                    self.send(out, land, self.ssem.at[0], sem, way).start()

    def result(self):
        rows = []
        for p in range(len(self.pieces)):
            value = self.own[self.me, pl.ds(*self.pieces[p])]
            for way in (1, -1):
                if p in self.of(way, self.n == 2):
                    value = value + self.arrived(way, self.n // 2 - 1, p)
            rows.append(value)
        return jnp.concatenate(rows, axis=0)


def kernel(
    cfg,
    x_hbm, pre_hbm, w_in_hbm, w_out_hbm, og_hbm, swap_hbm, unfold_hbm, fold_hbm,
    ig_hbm, wi_hbm, bi_hbm, wo_hbm, bo_hbm,
    x_ref, og_ref, ig_ref, wi, bi_ref, wo, bo_ref,
    w_in, w_out, swap, unfold, fold, sb, rb, gg, ii, gy, pre, hid, slope, pb, pr, act, actz, sx, sr, sc, tb, tr,
    fb, qq,
    loc, outs, s_pre, r_pre, s1, r1, sg, rg, si, ri, sp, rp, sa, ra, ss, rs, st, rt, sq, rq,
):
    N, X, zl_n = cfg["N"], cfg["X"], cfg["ZL"]
    U = 2 * N * T
    H = cfg["H"]
    W = cfg["W"]
    HF = STEPS * W
    M = N * U
    RB = M // X
    UR = RB // U
    TK = 2 * zl_n * T

    tok, x, col = lax.axis_index("tok"), lax.axis_index("row"), lax.axis_index("col")
    y, c = lax.rem(tok, N), lax.rem(col, 2)
    z = (tok // N) * zl_n + col // 2
    b = y + c * (z - y)
    a = z + c * (y - z)

    def dev(yy, zz, cc, xx=x):
        return ((zz // zl_n) * N + yy, xx, lax.rem(zz, zl_n) * 2 + cc)

    def bdev(bb):
        return dev(y + (1 - c) * (bb - y), z + c * (bb - z), c)

    def adev(aa, cc):
        return dev(y + c * (aa - y), z + (1 - c) * (aa - z), cc)

    def xdev(xx):
        return dev(y, z, c, xx)

    mate = dev(y, z, 1 - c)

    def rcopy(src, dst, ssem, rsem, to):
        return pltpu.make_async_remote_copy(
            src_ref=src, dst_ref=dst, send_sem=ssem, recv_sem=rsem, device_id=to, device_id_type=MESH
        )

    def along_b(src, dst, ssem, rsem, way):
        to = mate if way == 0 else bdev(lax.rem(b + way + N, N))
        return rcopy(src, dst, ssem, rsem, to)

    def along_x(src, dst, ssem, rsem, way):
        return rcopy(src, dst, ssem, rsem, xdev(lax.rem(x + way + X, X)))

    def got(dst, rsem):
        rcopy(dst, dst, rsem, rsem, mate).wait_recv()

    def sent(src, ssem):
        rcopy(src, src, ssem, ssem, mate).wait_send()

    loads = [
        pltpu.make_async_copy(pre_hbm, pre.at[x], loc.at[0]),
        pltpu.make_async_copy(unfold_hbm, unfold, loc.at[1]),
        pltpu.make_async_copy(swap_hbm, swap, loc.at[2]),
        pltpu.make_async_copy(w_out_hbm, w_out, loc.at[3]),
        pltpu.make_async_copy(w_in_hbm, w_in, loc.at[4]),
        pltpu.make_async_copy(fold_hbm, fold, loc.at[5]),
    ]
    tokens = (pltpu.make_async_copy(og_hbm, og_ref, loc.at[6]), pltpu.make_async_copy(x_hbm, x_ref, loc.at[7]))
    for load in tokens:
        load.start()

    stores = []

    def put(src, dst):
        stores.append(pltpu.make_async_copy(src, dst, outs.at[len(stores)]))
        stores[-1].start()

    bar = pltpu.get_barrier_semaphore()

    def greet(yy, zz, cc, xx=x):
        pl.semaphore_signal(bar, inc=1, device_id=dev(yy, zz, cc, xx), device_id_type=MESH)

    greet(y, z, 1 - c)
    for d in range(1, X):
        greet(y, z, c, lax.rem(x + d, X))

    def greet_step(d, _):
        yy, zz = lax.rem(y + d, N), lax.rem(z + d, N)
        for cc in range(2):
            greet(yy, z, cc)
            greet(y, zz, cc)
        return 0

    lax.fori_loop(1, N, greet_step, 0)

    for load in loads:
        load.start()

    for load in tokens:
        load.wait()
    og = og_ref[...].astype(F32)
    xall = x_ref[...].astype(F32)
    xs = xall[0:T]
    for k in range(1, 2 * zl_n):
        xs = jnp.where(col == k, xall[T * k : T * k + T], xs)
    pad = jnp.zeros((1, W), F32)
    for k, v in enumerate((og, xs)):
        for h in range(2):
            rows = [v[:, h * HF + j * W : h * HF + (j + 1) * W] for j in range(STEPS)] + [pad]
            sb[k, h] = jnp.concatenate(rows, axis=0).astype(BF16)

    pl.semaphore_wait(bar, 1 + (X - 1) + 4 * (N - 1))

    def small_phase(k):
        @pl.when(c == 0)
        def _():
            rb[k, 2 * z] = sb[k, 0]
            rcopy(sb.at[k, 1], rb.at[k, 2 * y], s1.at[k], r1.at[k], mate).start()

        @pl.when(c == 1)
        def _():
            rb[k, 2 * y + 1] = sb[k, 1]
            rcopy(sb.at[k, 0], rb.at[k, 2 * z + 1], s1.at[k], r1.at[k], mate).start()

        def small(d, _):
            yy, zz = lax.rem(y + d, N), lax.rem(z + d, N)
            rcopy(sb.at[k, 0], rb.at[k, 2 * z + c], s1.at[k], r1.at[k], dev(y, zz, 0)).start()
            rcopy(sb.at[k, 1], rb.at[k, 2 * y + c], s1.at[k], r1.at[k], dev(yy, z, 1)).start()
            return 0

        lax.fori_loop(1, N, small, 0)

    def unit_of(k, buf):
        got(rb.at[k, pl.ds(0, 2 * N - 1)], r1.at[k])
        unit = nn(unfold[...], rb[k].reshape(2 * N * 16, W)).astype(BF16)
        for j in range(STEPS):
            buf[c * N + b, :, j * W : (j + 1) * W] = unit[j * U : j * U + U]

    small_phase(0)

    for d in range(1, X):
        rcopy(pre_hbm, pre.at[x], s_pre.at[0], r_pre.at[x], xdev(lax.rem(x + d, X))).start()

    def gelu_block(r):
        for q in range(RB // TK):
            g = r * (RB // TK) + q
            zh, yy = g // N, lax.rem(g, N)
            rows = pl.ds(pl.multiple_of(yy * U + zh * TK, 8), TK)
            result, grade = gelu_parts(pre[r].astype(F32)[q * TK : q * TK + TK])
            hid[rows] = result
            slope[rows] = grade

    loads[0].wait()
    gelu_block(x)
    loads[1].wait()
    pieces = cfg["pieces"]
    grads = Gather(N, b, gg, lambda u: c * N + u, pieces, sg, rg, along_b, True)
    xs_ring = Gather(N, b, ii, lambda u: c * N + u, pieces, si, ri, along_b, True)
    unit_of(0, gg)
    grads.start()
    small_phase(1)

    def from_mate(ring):
        def step(k, _):
            for p in range(len(pieces)):
                at = (1 - c) * N + k
                got(ring.buf.at[at, pl.ds(*pieces[p])], ring.rsem.at[at * len(pieces) + p])
            return 0

        lax.fori_loop(0, N, step, 0)

    for k in range(1, N // 2 + 1):
        grads.step(k)
        if k < X:
            r = lax.rem(x + k, X)
            got(pre.at[r], r_pre.at[r])
            gelu_block(r)
    for k in range(N // 2 + 1, X):
        r = lax.rem(x + k, X)
        got(pre.at[r], r_pre.at[r])
        gelu_block(r)
    unit_of(1, ii)
    xs_ring.start()
    for load in loads[2:]:
        load.wait()
    from_mate(grads)

    def part(r):
        g1 = gg[pl.ds(N, N)].reshape(M, HF)
        mine = pl.ds(pl.multiple_of(r * RB, 16), RB)
        g1y = nn(swap[mine], g1).astype(BF16)
        gy[mine] = g1y
        g0 = gg[pl.ds(r * UR, UR)].reshape(RB, HF)
        return nt(g0, w_out[:, :HF]) + nt(g1y, w_out[:, HF:])

    def steps(n, me):
        return [n // 2] + [v for s in range(1, n // 2) for v in (n // 2 - s, n // 2 + s)] + [0]

    later = list(range(1, N // 2 + 1))

    def more():
        if later:
            xs_ring.step(later.pop(0))

    CH = RB // CHUNKS
    for v in steps(X, x)[:-1]:
        r = lax.rem(x + v, X)
        value = part(r).astype(BF16)
        for q in range(CHUNKS):
            pb[q, r] = value[q * CH : q * CH + CH]
            rcopy(pb.at[q, r], pr.at[q, x], sp.at[0], rp.at[q], xdev(r)).start()
    mine = part(x)

    hidden = hid[...].astype(BF16)
    more()
    wo[:, :HF] = tn(hidden, gg[pl.ds(0, N)].reshape(M, HF)).astype(BF16)
    for q in range(CHUNKS):
        got(pr.at[q, pl.ds(0, X - 1)], rp.at[q])
        total = mine[q * CH : q * CH + CH]
        for v in range(1, X):
            total = total + pr[q, lax.rem(x + v, X)].astype(F32)
        rows = pl.ds(pl.multiple_of(x * RB + q * CH, 16), CH)
        act[x, q * CH : q * CH + CH] = (total * slope[rows]).astype(BF16)
        piece = act.at[x, pl.ds(q * CH, CH)]
        for v in steps(X, x)[:-1]:
            rcopy(piece, piece, sa.at[0], ra.at[0], xdev(lax.rem(x + v, X))).start()
    more()
    wo[:, HF:] = tn(hidden, gy[...]).astype(BF16)
    put(wo, wo_hbm)
    got(act.at[pl.ds(0, X - 1)], ra.at[0])
    acty = act[...].reshape(M, H)
    actz[0] = acty.reshape(N, U, H)
    actz[1] = nn(swap[...], acty).astype(BF16).reshape(N, U, H)
    more()

    mate_b = z + c * (y - z)
    order = steps(N, b)
    pairs = [order[i : i + 2] for i in range(0, N, 2)]

    def product(h, base, pair):
        units = [lax.rem(base + v, N) for v in pair]
        rows = jnp.concatenate([actz[h, u] for u in units], axis=0)
        return units, nt(rows, w_in[h])

    def for_mate(i):
        units, value = product(1 - c, mate_b, pairs[i])
        for k, u in enumerate(units):
            sx[u] = value[k * U : k * U + U].astype(BF16)
            rcopy(sx.at[u], sr.at[u], ss.at[0], rs.at[u], mate).start()

    def for_me(i):
        units, value = product(c, b, pairs[i])
        for k, u in enumerate(units):
            got(sr.at[u], rs.at[u])
            sc[u] = value[k * U : k * U + U] + sr[u].astype(F32)

    sums = Scatter(N, b, sc, tb, tr, pieces, st, rt, along_b)
    done = 0
    for_mate(0)
    for i in range(len(pairs)):
        if i + 1 < len(pairs):
            for_mate(i + 1)
        for_me(i)
        while done < N // 2 and (2 * done + 1) < 2 * (i + 1):
            if done == i:
                sums.step(done)
                done += 1
            else:
                break
    while later:
        more()
    while done < N // 2:
        sums.step(done)
        done += 1
    from_mate(xs_ring)
    bo = [jnp.sum(v.astype(F32), axis=0, keepdims=True) for v in (gg[pl.ds(0, N)].reshape(M, HF), gy[...])]
    bo_ref[...] = jnp.concatenate(bo, axis=1).reshape(bo_ref.shape)
    put(bo_ref, bo_hbm)
    bi_ref[...] = jnp.sum(act[...].reshape(M, H).astype(F32), axis=0, keepdims=True).reshape(bi_ref.shape)
    put(bi_ref, bi_hbm)
    for h in range(2):
        wi[h] = tn(ii[pl.ds(h * N, N)].reshape(M, HF), actz[h].reshape(M, H)).astype(BF16)
    put(wi, wi_hbm)

    total = sums.result().astype(BF16)
    stack = jnp.concatenate([total[:, j * W : (j + 1) * W] for j in range(STEPS)], axis=0)
    fb[...] = nn(fold[...], stack).astype(BF16).reshape(2 * N, 16, W)
    slot = c * N + a
    qq[slot] = fb[2 * a + c]
    rcopy(fb.at[2 * a + 1 - c], qq.at[slot], sq.at[0], rq.at[0], mate).start()

    def last(d, _):
        aa = lax.rem(a + d, N)
        for cc in range(2):
            rcopy(fb.at[2 * aa + cc], qq.at[slot], sq.at[0], rq.at[0], adev(aa, cc)).start()
        return 0

    lax.fori_loop(1, N, last, 0)
    got(qq.at[pl.ds(0, 2 * N - 1)], rq.at[0])
    for h in range(2):
        rows = jnp.sum(qq[pl.ds(h * N, N)].astype(F32), axis=0)
        for j in range(STEPS):
            at = h * HF + j * W
            ig_ref[:, at : at + W] = rows[T * j : T * j + T].astype(BF16)
    put(ig_ref, ig_hbm)

    for k in range(2):
        sent(rb.at[k, pl.ds(0, 2 * N - 1)], s1.at[k])
    sent(pre.at[pl.ds(0, X - 1)], s_pre.at[0])
    sent(gg.at[pl.ds(0, 2 * N - 1)], sg.at[0])
    sent(ii.at[pl.ds(0, 2 * N - 1)], si.at[0])
    sent(pb.at[:, pl.ds(0, X - 1)], sp.at[0])
    sent(act.at[pl.ds(0, X - 1)], sa.at[0])
    sent(sx, ss.at[0])
    sent(tb.at[pl.ds(0, N - 1)], st.at[0])
    sent(qq.at[pl.ds(0, 2 * N - 1)], sq.at[0])
    for copy in stores:
        copy.wait()


def finish(*refs):
    srcs, dsts, held, sem = refs[:5], refs[5:10], refs[10:15], refs[15]
    moves = []
    for src, dst, mid in zip(srcs, dsts, held):
        cuts = 4 if len(src.shape) == 2 and src.shape[0] > 64 else 1
        rows = src.shape[0] // cuts
        for k in range(cuts):
            piece = pl.ds(k * rows, rows)
            one, two, three = (r.at[piece] if cuts > 1 else r for r in (src, mid, dst))
            n = 2 * len(moves)
            moves.append((pltpu.make_async_copy(one, two, sem.at[n]), pltpu.make_async_copy(two, three, sem.at[n + 1])))
            moves[-1][0].start()
    for load, store in moves:
        load.wait()
        store.start()
    for load, store in moves:
        store.wait()


def tables(n, u):
    m = n * u
    q = 2 * T
    r = np.arange(m)
    swap = np.zeros((m, m), np.float32)
    swap[r, ((r % u) // q) * u + (r // u) * q + r % q] = 1
    fold = np.zeros((2 * n * 16, STEPS * u), np.float32)
    for j in range(STEPS):
        for t in range(u):
            fold[(t // T) * 16 + T * j + t % T, j * u + t] = 1
    return swap, fold.T, fold


def make_body(X, N, zl_n):
    U = 2 * N * T
    M = N * U

    def body(inputs, pre_act, w_in, w_out, out_grad):
        F, H = w_in.shape
        W = F // (2 * STEPS)
        HF = F // 2
        RB = M // X
        pieces = tuple((at, U // 5) for at in range(0, U, U // 5))
        np_ = len(pieces)
        cfg = {"N": N, "X": X, "ZL": zl_n, "H": H, "W": W, "pieces": pieces}
        consts = [jnp.asarray(t, BF16) for t in tables(N, U)]
        held = [pltpu.VMEM(s, t) for s, t in (((T, F), BF16), ((F, H), BF16), ((H,), F32), ((H, F), BF16), ((F,), F32))]
        hbm = pl.BlockSpec(memory_space=pltpu.HBM)
        dma = pltpu.SemaphoreType.DMA
        outs = pl.pallas_call(
            functools.partial(kernel, cfg),
            out_shape=(
                jax.ShapeDtypeStruct((T, F), BF16),
                jax.ShapeDtypeStruct((2, HF, H), BF16),
                jax.ShapeDtypeStruct((H,), F32),
                jax.ShapeDtypeStruct((H, F), BF16),
                jax.ShapeDtypeStruct((F,), F32),
            ),
            in_specs=[hbm] * 8,
            out_specs=(hbm,) * 5,
            scratch_shapes=[
                pltpu.VMEM(inputs.shape, BF16),
                pltpu.VMEM(out_grad.shape, BF16),
                pltpu.VMEM((T, F), BF16),
                pltpu.VMEM((2, HF, H), BF16),
                pltpu.VMEM((H,), F32),
                pltpu.VMEM((H, F), BF16),
                pltpu.VMEM((F,), F32),
                pltpu.VMEM((2, HF, H), BF16),
                pltpu.VMEM((H, F), BF16),
                pltpu.VMEM(consts[0].shape, BF16),
                pltpu.VMEM(consts[1].shape, BF16),
                pltpu.VMEM(consts[2].shape, BF16),
                pltpu.VMEM((2, 2, 16, W), BF16),
                pltpu.VMEM((2, 2 * N, 16, W), BF16),
                pltpu.VMEM((2 * N, U, HF), BF16),
                pltpu.VMEM((2 * N, U, HF), BF16),
                pltpu.VMEM((M, HF), BF16),
                pltpu.VMEM((X, RB, H), BF16),
                pltpu.VMEM((M, H), F32),
                pltpu.VMEM((M, H), F32),
                pltpu.VMEM((CHUNKS, X, RB // CHUNKS, H), BF16),
                pltpu.VMEM((CHUNKS, X, RB // CHUNKS, H), BF16),
                pltpu.VMEM((X, RB, H), BF16),
                pltpu.VMEM((2, N, U, H), BF16),
                pltpu.VMEM((N, U, HF), BF16),
                pltpu.VMEM((N, U, HF), BF16),
                pltpu.VMEM((N, U, HF), F32),
                pltpu.VMEM((N, U, HF), BF16),
                pltpu.VMEM((N, U, HF), BF16),
                pltpu.VMEM((2 * N, 16, W), BF16),
                pltpu.VMEM((2 * N, 16, W), BF16),
                dma((8,)), dma((5,)),
                dma((1,)), dma((X,)),
                dma((2,)), dma((2,)),
                dma((1,)), dma((2 * N * np_,)),
                dma((1,)), dma((2 * N * np_,)),
                dma((1,)), dma((CHUNKS,)),
                dma((1,)), dma((1,)),
                dma((1,)), dma((N,)),
                dma((1,)), dma((N * np_,)),
                dma((1,)), dma((1,)),
            ],
            compiler_params=pltpu.CompilerParams(
                collective_id=0, has_side_effects=True, vmem_limit_bytes=VM
            ),
        )(inputs, pre_act, w_in.reshape(2, HF, H), w_out, out_grad, *consts)
        ig, wi, bi, wo, bo = outs
        return pl.pallas_call(
            finish,
            out_shape=(
                jax.ShapeDtypeStruct((T, F), BF16),
                jax.ShapeDtypeStruct((F, H), BF16),
                jax.ShapeDtypeStruct((H,), F32),
                jax.ShapeDtypeStruct((H, F), BF16),
                jax.ShapeDtypeStruct((F,), F32),
            ),
            in_specs=[hbm] * 5,
            out_specs=(hbm,) * 5,
            scratch_shapes=[*held, dma((22,))],
            compiler_params=pltpu.CompilerParams(vmem_limit_bytes=VM),
        )(ig, wi.reshape(F, H), bi, wo, bo)

    return body


def solution(mesh):
    zl_n = mesh.shape["col"] // 2
    body = make_body(mesh.shape["row"], math.isqrt(mesh.shape["tok"] * zl_n), zl_n)
    return jax.shard_map(
        body,
        mesh=mesh,
        in_specs=(
            P("tok", "row"),
            P("row", ("tok", "col")),
            P("row", ("tok", "col")),
            P(("tok", "col"), "row"),
            P(("tok", "col"), "row"),
        ),
        out_specs=(
            P(("tok", "col"), "row"),
            P("row", ("tok", "col")),
            P(("tok", "col")),
            P(("tok", "col"), "row"),
            P("row"),
        ),
        check_vma=False,
    )
```

time: 89.2 us -> 78.4 us (0.88)
  local copies, waits for them, and re-layouts: 4.86 us -> 0 us
  Pallas kernels: 80.9 us -> 77.6 us
  other arithmetic: 2.57 us -> 0 us
    pallas_call x1, Pallas kernels: 80.9 us -> 75 us  [body(): pl.pallas_call(functools.partial(kernel, cfg), out_shape=(jax.ShapeDtypeS...]
    unnamed x5 -> x0, local copies, waits for them, and re-layouts: 4.86 us -> none
    pallas_call x0 -> x1, Pallas kernels: none -> 2.57 us  [body(): pl.pallas_call(finish, out_shape=(jax.ShapeDtypeStruct((T, F), BF16), jax...]
    pallas_call x2 -> x0, other arithmetic: 2.57 us -> none  [body(): pl.pallas_call(functools.partial(kernel, cfg), out_shape=(jax.ShapeDtypeS...]
where the time goes in v2:
time: 78.4 us; the launch traced here: 78.2 us
  Pallas kernels  77.6 us (99%)
    pallas_call x1, Pallas kernels, body(): pl.pallas_call(functools.partial(kernel, cfg), out_shape=(jax.ShapeDtypeS...  75 us
    pallas_call x1, Pallas kernels, body(): pl.pallas_call(finish, out_shape=(jax.ShapeDtypeStruct((T, F), BF16), jax...  2.57 us

profile of v2, /device:TPU:1, one launch (start us, length us, event | category | flops | bytes accessed | tf_op | source)
XLA Modules:
  0.0 78.2 jit_solution(4221341594689864363)
XLA Ops:
  0.6 75.0 %shard_map.119 = (bf16[5,1536]{1,0:T(8,128)(2,1)}, bf16[2,768,384]{2,1,0:T(8,128)(2,1)}, f32[384]{0:T(512)}, bf16[384,1536]{1,0:T(8,128)(2,1)}, f32[1536]{0:T(1024)}) custom-call(bf16[40,1536]{1,0:T(8,128)(2,1)} %x_hbm.1, bf16[160,384]{1,0:T(8,128)(2,1)} %pre_hbm.1, bf16[2,768,384]{2,1,0:T(8,128)(2,1)} %bitcast.2, bf16[384,1536]{1,0:T(8,128)(2,1)} %w_out_hbm.1, ...), custom_call_target="tpu_custom_call" | custom-call | tf_op jit(solution)/shard_map/pallas_call | solution.py:495
  75.7 2.6 %shard_map.120 = (bf16[5,1536]{1,0:T(8,128)(2,1)}, bf16[1536,384]{1,0:T(8,128)(2,1)}, f32[384]{0:T(512)}, bf16[384,1536]{1,0:T(8,128)(2,1)}, f32[1536]{0:T(1024)}) custom-call(bf16[5,1536]{1,0:T(8,128)(2,1)} %get-tuple-element.10.refs_0_, bf16[1536,384]{1,0:T(8,128)(2,1)} %bitcast.3, f32[384]{0:T(512)} %get-tuple-element.12.refs_2_, ...), custom_call_target="tpu_custom_call" | custom-call | tf_op jit(solution)/shard_map/pallas_call | solution.py:554

commit v3 on v2

--- a/solution.py
+++ b/solution.py
@@ -44,9 +44,10 @@
 
 
 class Gather:
-    def __init__(self, n, me, buf, slot, pieces, ssem, rsem, send, mate):
+    def __init__(self, n, me, buf, slot, pieces, ssem, rsem, msem, send):
         self.n, self.me, self.buf, self.slot, self.pieces = n, me, buf, slot, pieces
-        self.ssem, self.rsem, self.send, self.mate = ssem, rsem, send, mate
+        self.ssem, self.rsem, self.msem, self.send = ssem, rsem, msem, send
+        self.all = range(len(pieces))
 
     def piece(self, unit, p):
         at, size = self.pieces[p]
@@ -54,47 +55,44 @@
 
     def push(self, unit, p, to):
         ref, sem = self.piece(unit, p)
-        self.send(ref, ref, self.ssem.at[0], sem, to).start()
-
-    def of(self, way, far):
-        half = (len(self.pieces) + 1) // 2
-        every = range(len(self.pieces))
-        return every if not far else (every[:half] if way > 0 else every[half:])
+        self.send(ref, ref, self.ssem.at[0], sem if to else self.msem.at[0], to).start()
+
+    def far(self, way, p):
+        return (p < (len(self.pieces) + 1) // 2) == (way > 0)
 
     def start(self):
-        for p in range(len(self.pieces)):
+        for hop in (2, 1):
+            for p in self.all:
+                for way in (1, -1):
+                    self.push(self.me, p, way * hop)
+        for p in self.all:
+            self.push(self.me, p, 0)
+
+    def step(self, k):
+        for p in self.all:
             for way in (1, -1):
-                if p in self.of(way, self.n == 2):
-                    self.push(self.me, p, way)
-        if self.mate:
-            for p in range(len(self.pieces)):
-                self.push(self.me, p, 0)
-
-    def step(self, k):
-        for p in range(len(self.pieces)):
-            for way in (1, -1):
-                if p in self.of(way, 2 * k == self.n):
+                if k < 4 or self.far(way, p):
                     unit = lax.rem(self.me - way * k + self.n, self.n)
                     ref, sem = self.piece(unit, p)
                     self.send(ref, ref, sem, sem, 0).wait_recv()
-                    if 2 * k < self.n and p in self.of(way, 2 * k + 2 == self.n):
+                    if k == 2:
+                        if self.far(way, p):
+                            self.push(unit, p, 2 * way)
                         self.push(unit, p, way)
-                    if self.mate:
-                        self.push(unit, p, 0)
+                    self.push(unit, p, 0)
 
 
 class Scatter:
     def __init__(self, n, me, own, out, land, pieces, ssem, rsem, send):
         self.n, self.me, self.own, self.out, self.land, self.pieces = n, me, own, out, land, pieces
         self.ssem, self.rsem, self.send = ssem, rsem, send
-
-    def of(self, way, first):
-        half = (len(self.pieces) + 1) // 2
-        every = range(len(self.pieces))
-        return every if not first else (every[:half] if way > 0 else every[half:])
+        self.all = range(len(pieces))
+
+    def far(self, way, p):
+        return (p < (len(self.pieces) + 1) // 2) == (way > 0)
 
     def place(self, way, s, p):
-        at = (0 if way > 0 else self.n // 2) + s
+        at = (0 if way > 0 else 4) + s
         rows = pl.ds(*self.pieces[p])
         return self.out.at[at, rows], self.land.at[at, rows], self.rsem.at[at * len(self.pieces) + p]
 
@@ -103,25 +101,26 @@
         self.send(land, land, sem, sem, 0).wait_recv()
         return land[...].astype(F32)
 
-    def step(self, s):
-        for p in range(len(self.pieces)):
-            for way in (1, -1):
-                if p in self.of(way, s == 0):
-                    unit = lax.rem(self.me + way * (self.n // 2 - s) + self.n, self.n)
-                    value = self.own[unit, pl.ds(*self.pieces[p])]
-                    if s and p in self.of(way, s == 1):
-                        value = value + self.arrived(way, s - 1, p)
-                    out, land, sem = self.place(way, s, p)
-                    out[...] = value.astype(BF16)
-                    self.send(out, land, self.ssem.at[0], sem, way).start()
+    def step(self, s, way):
+        unit = lax.rem(self.me + way * (4, 3, 1, 2)[s] + self.n, self.n)
+        for p in self.all:
+            if s or self.far(way, p):
+                value = self.own[unit, pl.ds(*self.pieces[p])]
+                if s == 3:
+                    value = value + self.arrived(way, 1, p)
+                    if self.far(way, p):
+                        value = value + self.arrived(way, 0, p)
+                out, land, sem = self.place(way, s, p)
+                out[...] = value.astype(BF16)
+                self.send(out, land, self.ssem.at[0], sem, way * (2, 1, 1, 2)[s]).start()
 
     def result(self):
         rows = []
-        for p in range(len(self.pieces)):
+        for p in self.all:
             value = self.own[self.me, pl.ds(*self.pieces[p])]
-            for way in (1, -1):
-                if p in self.of(way, self.n == 2):
-                    value = value + self.arrived(way, self.n // 2 - 1, p)
+            for s in (2, 3):
+                for way in (1, -1):
+                    value = value + self.arrived(way, s, p)
             rows.append(value)
         return jnp.concatenate(rows, axis=0)
 
@@ -133,7 +132,7 @@
     x_ref, og_ref, ig_ref, wi, bi_ref, wo, bo_ref,
     w_in, w_out, swap, unfold, fold, sb, rb, gg, ii, gy, pre, hid, slope, pb, pr, act, actz, sx, sr, sc, tb, tr,
     fb, qq,
-    loc, outs, s_pre, r_pre, s1, r1, sg, rg, si, ri, sp, rp, sa, ra, ss, rs, st, rt, sq, rq,
+    loc, outs, s_pre, r_pre, s1, r1, sg, rg, mg, si, ri, mi, sp, rp, sa, ra, ss, rs, st, rt, sq, rq,
 ):
     N, X, zl_n = cfg["N"], cfg["X"], cfg["ZL"]
     U = 2 * N * T
@@ -280,20 +279,14 @@
     gelu_block(x)
     loads[1].wait()
     pieces = cfg["pieces"]
-    grads = Gather(N, b, gg, lambda u: c * N + u, pieces, sg, rg, along_b, True)
-    xs_ring = Gather(N, b, ii, lambda u: c * N + u, pieces, si, ri, along_b, True)
+    grads = Gather(N, b, gg, lambda u: c * N + u, pieces, sg, rg, mg, along_b)
+    xs_ring = Gather(N, b, ii, lambda u: c * N + u, pieces, si, ri, mi, along_b)
     unit_of(0, gg)
     grads.start()
     small_phase(1)
 
     def from_mate(ring):
-        def step(k, _):
-            for p in range(len(pieces)):
-                at = (1 - c) * N + k
-                got(ring.buf.at[at, pl.ds(*pieces[p])], ring.rsem.at[at * len(pieces) + p])
-            return 0
-
-        lax.fori_loop(0, N, step, 0)
+        got(ring.buf.at[pl.ds((1 - c) * N, N)], ring.msem.at[0])
 
     for k in range(1, N // 2 + 1):
         grads.step(k)
@@ -305,8 +298,6 @@
         r = lax.rem(x + k, X)
         got(pre.at[r], r_pre.at[r])
         gelu_block(r)
-    unit_of(1, ii)
-    xs_ring.start()
     for load in loads[2:]:
         load.wait()
     from_mate(grads)
@@ -337,8 +328,9 @@
             rcopy(pb.at[q, r], pr.at[q, x], sp.at[0], rp.at[q], xdev(r)).start()
     mine = part(x)
 
+    unit_of(1, ii)
+    xs_ring.start()
     hidden = hid[...].astype(BF16)
-    more()
     wo[:, :HF] = tn(hidden, gg[pl.ds(0, N)].reshape(M, HF)).astype(BF16)
     for q in range(CHUNKS):
         got(pr.at[q, pl.ds(0, X - 1)], rp.at[q])
@@ -353,11 +345,11 @@
     more()
     wo[:, HF:] = tn(hidden, gy[...]).astype(BF16)
     put(wo, wo_hbm)
+    more()
     got(act.at[pl.ds(0, X - 1)], ra.at[0])
     acty = act[...].reshape(M, H)
     actz[0] = acty.reshape(N, U, H)
     actz[1] = nn(swap[...], acty).astype(BF16).reshape(N, U, H)
-    more()
 
     mate_b = z + c * (y - z)
     order = steps(N, b)
@@ -381,23 +373,23 @@
             sc[u] = value[k * U : k * U + U] + sr[u].astype(F32)
 
     sums = Scatter(N, b, sc, tb, tr, pieces, st, rt, along_b)
-    done = 0
     for_mate(0)
-    for i in range(len(pairs)):
-        if i + 1 < len(pairs):
-            for_mate(i + 1)
-        for_me(i)
-        while done < N // 2 and (2 * done + 1) < 2 * (i + 1):
-            if done == i:
-                sums.step(done)
-                done += 1
-            else:
-                break
+    for_mate(1)
+    for_me(0)
+    for s, way in ((0, 1), (0, -1), (1, 1)):
+        sums.step(s, way)
+    for_mate(2)
+    for_me(1)
+    sums.step(1, -1)
+    for_mate(3)
+    for_me(2)
+    sums.step(2, 1)
+    for_me(3)
+    sums.step(2, -1)
+    sums.step(3, 1)
+    sums.step(3, -1)
     while later:
         more()
-    while done < N // 2:
-        sums.step(done)
-        done += 1
     from_mate(xs_ring)
     bo = [jnp.sum(v.astype(F32), axis=0, keepdims=True) for v in (gg[pl.ds(0, N)].reshape(M, HF), gy[...])]
     bo_ref[...] = jnp.concatenate(bo, axis=1).reshape(bo_ref.shape)
@@ -485,7 +477,7 @@
         W = F // (2 * STEPS)
         HF = F // 2
         RB = M // X
-        pieces = tuple((at, U // 5) for at in range(0, U, U // 5))
+        pieces = ((0, U * 3 // 5), (U * 3 // 5, U * 2 // 5))
         np_ = len(pieces)
         cfg = {"N": N, "X": X, "ZL": zl_n, "H": H, "W": W, "pieces": pieces}
         consts = [jnp.asarray(t, BF16) for t in tables(N, U)]
@@ -538,8 +530,8 @@
                 dma((8,)), dma((5,)),
                 dma((1,)), dma((X,)),
                 dma((2,)), dma((2,)),
-                dma((1,)), dma((2 * N * np_,)),
-                dma((1,)), dma((2 * N * np_,)),
+                dma((1,)), dma((2 * N * np_,)), dma((1,)),
+                dma((1,)), dma((2 * N * np_,)), dma((1,)),
                 dma((1,)), dma((CHUNKS,)),
                 dma((1,)), dma((1,)),
                 dma((1,)), dma((N,)),

time: 78.4 us -> 72.6 us (0.926)
  Pallas kernels: 77.6 us -> 71.8 us
    pallas_call x1, Pallas kernels: 75 us -> 69.2 us  [body(): pl.pallas_call(functools.partial(kernel, cfg), out_shape=(jax.ShapeDtypeS...]
where the time goes in v3:
time: 72.6 us; the launch traced here: 72.4 us
  Pallas kernels  71.8 us (99%)
    pallas_call x1, Pallas kernels, body(): pl.pallas_call(functools.partial(kernel, cfg), out_shape=(jax.ShapeDtypeS...  69.2 us
    pallas_call x1, Pallas kernels, body(): pl.pallas_call(finish, out_shape=(jax.ShapeDtypeStruct((T, F), BF16), jax...  2.57 us

profile of v3, /device:TPU:1, one launch (start us, length us, event | category | flops | bytes accessed | tf_op | source)
XLA Modules:
  0.0 72.4 jit_solution(12598083648958557315)
XLA Ops:
  0.6 69.2 %shard_map.119 = (bf16[5,1536]{1,0:T(8,128)(2,1)}, bf16[2,768,384]{2,1,0:T(8,128)(2,1)}, f32[384]{0:T(512)}, bf16[384,1536]{1,0:T(8,128)(2,1)}, f32[1536]{0:T(1024)}) custom-call(bf16[40,1536]{1,0:T(8,128)(2,1)} %x_hbm.1, bf16[160,384]{1,0:T(8,128)(2,1)} %pre_hbm.1, bf16[2,768,384]{2,1,0:T(8,128)(2,1)} %bitcast.2, bf16[384,1536]{1,0:T(8,128)(2,1)} %w_out_hbm.1, ...), custom_call_target="tpu_custom_call" | custom-call | tf_op jit(solution)/shard_map/pallas_call | solution.py:487
  69.9 2.6 %shard_map.120 = (bf16[5,1536]{1,0:T(8,128)(2,1)}, bf16[1536,384]{1,0:T(8,128)(2,1)}, f32[384]{0:T(512)}, bf16[384,1536]{1,0:T(8,128)(2,1)}, f32[1536]{0:T(1024)}) custom-call(bf16[5,1536]{1,0:T(8,128)(2,1)} %get-tuple-element.10.refs_0_, bf16[1536,384]{1,0:T(8,128)(2,1)} %bitcast.3, f32[384]{0:T(512)} %get-tuple-element.12.refs_2_, ...), custom_call_target="tpu_custom_call" | custom-call | tf_op jit(solution)/shard_map/pallas_call | solution.py:546
